TPU v7x, 512 devices: a whole 4x8x8 slice. The times are simulated.
512 devices in a mesh: row: 32 (over z, y_lo, core), col: 16 (over x, y_hi).
Axes of the slice: x: 4, y: 8 (y_hi: 4, y_lo: 2; y = y_hi * 2 + y_lo), z: 8, core: 2. Of those that a mesh axis runs over, the one named last changes fastest.
Arguments:
- trailing: float32 [2, 8192, 4, 4096], P(None, 'row', None, 'col'), may hold values from -6 to 6
- panel: float32 [2, 8192, 256], P(None, 'row', 'col'), may hold values from -1 to 1
- factor_inverse: float32 [256, 256], replicated, may hold values from -2 to 3, as said below
Outputs:
- updated: float32 [2, 8192, 4, 4096], P(None, 'row', None, 'col')
- factor_panel: float32 [2, 8192, 256], P(None, 'row', 'col')
Inputs may be any that keep to these rules, and one draw needn't show every extreme that they name: `factor_inverse`: lower triangular; diagonal entries between 1 and 3.
All inputs are finite; a program needn't handle non-finite values.
Results may differ from a plain program's by a relative error of at most 0.00007.
Values sent between devices are 32-bit elements; how exact they have to be, the bound alone decides.
No kernel may reach another device: no remote copies, remote signals or barrier semaphores. Data moves between devices by JAX's collectives and lax.ppermute only.
A program may use at most 64 MiB of HBM per device.

v0:
```python
import jax
import jax.numpy as jnp
from jax import lax
from jax.sharding import PartitionSpec as P


def spread(x, axis, root):
    mine = lax.axis_index(axis) == root
    return lax.psum(jnp.where(mine, x, jnp.zeros_like(x)), axis)


def solve_rows(column, factor_inverse):
    return jnp.einsum(
        "tbk,ik->tbi",
        column,
        factor_inverse,
        preferred_element_type=jnp.float32,
        precision=lax.Precision.HIGHEST,
    )


def on_device(trailing, panel, factor_inverse):
    tile = panel.shape[1]
    row_tiles = panel.shape[0]
    sliver = panel.shape[2]
    ratio = lax.axis_size("row") // lax.axis_size("col")
    position = lax.axis_index("col")
    full_rows = lax.all_gather(panel, "col", axis=2, tiled=True)
    own_factor = solve_rows(full_rows, factor_inverse)
    received = []
    for offset in range(ratio):
        root = offset * lax.axis_size("col") + position
        received.append(spread(own_factor, "row", root))
    col_factor = jnp.stack(received, axis=1).reshape(row_tiles * ratio, tile, tile)
    col_tiles = col_factor.shape[0]
    product = jnp.dot(
        own_factor.reshape(row_tiles * tile, tile),
        col_factor.reshape(col_tiles * tile, tile).T,
        preferred_element_type=jnp.float32,
        precision=lax.Precision.HIGHEST,
    )
    updated = trailing - product.reshape(row_tiles, tile, col_tiles, tile)
    factor_panel = lax.dynamic_slice_in_dim(own_factor, position * sliver, sliver, 2)
    return (updated, factor_panel)


def solution(mesh):
    in_specs = (P(None, "row", None, "col"), P(None, "row", "col"), P())
    out_specs = (P(None, "row", None, "col"), P(None, "row", "col"))
    return jax.shard_map(
        on_device, mesh=mesh, in_specs=in_specs, out_specs=out_specs, check_vma=False
    )
```

profile of v0, /device:TPU:1, one launch (start us, length us, event | category | flops | bytes accessed | tf_op | source)
XLA Modules:
  0.0 304.4 jit_solution(7169277705098461847)
XLA Ops:
  7.2 0.0 copy-start
  7.2 0.0 all-reduce.3.cloned.1.call-start
  7.2 42.6 %all_gather.3 = f32[2,256,256]{1,2,0:T(8,128)S(1)} all-gather(f32[2,256,16]{1,2,0:T(8,128)} %param.4), channel_id=1, replica_groups=mesh['row'=32,'col'=16] {'col'}, dimensions={2}, use_global_device_ids=true | all-gather | bytes 557056 | tf_op jit(solution)/shard_map/all_gather | solution.py:28
  49.8 0.0 copy-done
  49.8 0.6 fusion.1
  50.5 1.1 select_bitcast_fusion.1
  51.6 0.0 all-reduce.3.cloned.1.call-update
  51.6 0.6 constant_dynamic-slice_fusion
  52.2 235.9 %all-reduce.3.cloned.1.call-done = (f32[2,1,256,256]{2,3,0,1:T(8,128)}, f32[2,1,256,256]{2,3,0,1:T(8,128)}) async-done(((f32[2,1,256,256]{2,3,0,1:T(8,128)}, f32[2,1,256,256]{2,3,0,1:T(8,128)}), (f32[2,1,256,256]{2,3,0,1:T(8,128)}, f32[2,1,256,256]{2,3,0,1:T(8,128)})) %all-reduce.3.cloned.1.call-update) | async-done | bytes 1048592 | tf_op jit(solution)/shard_map/psum | solution.py:9
  288.1 1.3 pad_maximum_fusion
  289.4 0.3 copy.8
  289.7 5.2 %copy_subtract_fusion = f32[2,256,4,256]{3,1,2,0:T(8,128)S(1)} fusion(f32[2,256,4,256]{3,2,1,0:T(4,128)} %param.3, f32[4,256,256,1]{2,1,0,3:T(8,128)S(1)} %bitcast.17, f32[2,256,256]{1,2,0:T(8,128)S(1)} %fusion.1), kind=kOutput, calls=%fused_computation | convolution fusion | flops 1611137024 | bytes 5767168 | tf_op jit(solution)/shard_map/dot_general | solution.py:36
  294.9 2.7 copy.11
Async XLA Ops:
  7.2 42.7 %copy-start = (f32[256,256]{1,0:T(8,128)S(1)}, f32[256,256]{1,0:T(8,128)}, u32[]{:S(2)}) copy-start(f32[256,256]{1,0:T(8,128)} %param.5) | copy-start | bytes 786436
  7.2 280.9 %all-reduce.3.cloned.1.call-start = ((), (), s32[]{:S(2)}) async-start(), calls=%async_computation | async-start | bytes 2097152 | tf_op jit(solution)/shard_map/psum | solution.py:9
Sparse Core Ops, SparseCore 0:
  51.7 236.3 all-reduce.2
where the time goes:
time: 305 us; the launch traced here: 304 us
  waiting for transfers between devices  236 us (77%)
  blocking collectives  42.6 us (14%)
  between operations  14.1 us (5%)
  matrix products  5.82 us (2%)
  local copies, waits for them, and re-layouts  3.63 us (1%)
    psum x1, waiting for transfers between devices, spread(): return lax.psum(jnp.where(mine, x, jnp.zeros_like(x)), axis)  236 us
    all_gather x1, blocking collectives, on_device(): full_rows = lax.all_gather(panel, 'col', axis=2, tiled=True)  42.6 us
  transfers between devices with their start and end apart: 1, of which 1 were waited for; matrix products, arithmetic and copies ran while one was open for 0% of the time, Pallas kernels for 0%

commit v1 on v0

v1 whole, which is shorter than its diff:
```python
import functools

import jax
import jax.numpy as jnp
from jax import lax
from jax.experimental import pallas as pl
from jax.experimental.pallas import tpu as pltpu
from jax.sharding import Mesh
from jax.sharding import PartitionSpec as P

AXES = ("zg", "z0", "yl", "core", "x", "yh")
SIZES = (4, 2, 2, 2, 4, 4)
ROW, COL = AXES[:4], AXES[4:]


def place(zg, z0, yl, core, x, yh):
    at = 0
    for size, i in zip(SIZES, (zg, z0, yl, core, x, yh)):
        at = at * size + i
    return at


def to_columns():
    pairs = []
    for zg in range(4):
        for z0 in range(2):
            for yl in range(2):
                for core in range(2):
                    for x in range(4):
                        for yh in range(4):
                            z = 2 * zg + z0
                            to = (yh + z + 2 * core + yl + x) % 4
                            target = place(to, x // 2, x % 2, z // 4, z % 4, 2 * yl + core)
                            pairs.append((place(zg, z0, yl, core, x, yh), target))
    return pairs


def gather(block, axes, n):
    many = jnp.broadcast_to(block[None], (n,) + block.shape)
    return lax.all_to_all(many, axes, 0, 0, tiled=True)


def split(value):
    high = value.astype(jnp.bfloat16)
    low = (value - high.astype(jnp.float32)).astype(jnp.bfloat16)
    return high, low


def product(left, right):
    dot = functools.partial(jnp.dot, preferred_element_type=jnp.float32)
    return dot(left[0], right[0]) + (dot(left[0], right[1]) + dot(left[1], right[0]))


def own_kernel(at_ref, rows_ref, inverse_ref, high_ref, low_ref, panel_ref):
    inverse = split(inverse_ref[...])
    start = pl.multiple_of(at_ref[0] * 16, 16)
    for t in range(2):
        factor = product(inverse, split(rows_ref[:, t].reshape(256, 256)))
        high_ref[t], low_ref[t] = split(factor.T)
        panel_ref[t] = product(
            split(inverse_ref[pl.ds(start, 16), :]), split(rows_ref[:, t].reshape(256, 256))
        )


def update_kernel(at_ref, trailing_ref, high_ref, low_ref, mine_ref, other_ref, inverse_ref, out_ref, right_high, right_low):
    @pl.when((pl.program_id(0) == 0) & (pl.program_id(1) == 0))
    def _():
        inverse = split(inverse_ref[...])
        for ref, half in ((mine_ref, at_ref[1]), (other_ref, 1 - at_ref[1])):
            for t in range(2):
                factor = product(inverse, split(ref[:, t].reshape(256, 256)))
                high, low = split(factor)
                for part in range(2):
                    start = pl.multiple_of((part * 4 + t * 2 + half) * 128, 128)
                    right_high[:, pl.ds(start, 128)] = high[:, part * 128 : part * 128 + 128]
                    right_low[:, pl.ds(start, 128)] = low[:, part * 128 : part * 128 + 128]

    total = product((high_ref[0], low_ref[0]), (right_high[...], right_low[...]))
    rows = total.shape[0]
    out_ref[0] = trailing_ref[0] - total.reshape(rows, 8, 128)


def on_device(trailing, panel, factor_inverse):
    col = lax.axis_index(COL)
    core = lax.axis_index("core")
    at = jnp.stack([col, core]).astype(jnp.int32)
    sliver = jnp.swapaxes(panel, 1, 2)
    quarter = gather(sliver, ("yh",), 4)
    (quarter,) = lax.optimization_barrier((quarter,))
    sent = lax.ppermute(quarter, AXES, to_columns())
    own = gather(quarter, ("x",), 4)
    sent, own = lax.optimization_barrier((sent, own))
    mine = gather(sent, ("z0", "yl"), 4)
    own, mine = own.reshape(16, 2, 16, 256), mine.reshape(16, 2, 16, 256)
    other = lax.ppermute(mine, "core", [(0, 1), (1, 0)])

    smem = pl.BlockSpec(memory_space=pltpu.SMEM)
    vmem = pl.BlockSpec(memory_space=pltpu.VMEM)
    high, low, factor_panel = pl.pallas_call(
        own_kernel,
        out_shape=[
            jax.ShapeDtypeStruct((2, 256, 256), jnp.bfloat16),
            jax.ShapeDtypeStruct((2, 256, 256), jnp.bfloat16),
            jax.ShapeDtypeStruct((2, 16, 256), jnp.float32),
        ],
        in_specs=[smem, vmem, vmem],
        out_specs=[vmem, vmem, vmem],
        compiler_params=pltpu.CompilerParams(vmem_limit_bytes=32 * 1024 * 1024),
    )(at, own, factor_inverse)

    whole = trailing.reshape(2, 256, 4, 2, 128).swapaxes(2, 3).reshape(2, 256, 8, 128)
    rows = 128
    updated = pl.pallas_call(
        update_kernel,
        grid=(2, 256 // rows),
        out_shape=jax.ShapeDtypeStruct((2, 256, 8, 128), jnp.float32),
        in_specs=[
            smem,
            pl.BlockSpec((1, rows, 8, 128), lambda t, i: (t, i, 0, 0)),
            pl.BlockSpec((1, rows, 256), lambda t, i: (t, i, 0)),
            pl.BlockSpec((1, rows, 256), lambda t, i: (t, i, 0)),
            vmem,
            vmem,
            vmem,
        ],
        out_specs=pl.BlockSpec((1, rows, 8, 128), lambda t, i: (t, i, 0, 0)),
        scratch_shapes=[
            pltpu.VMEM((256, 1024), jnp.bfloat16),
            pltpu.VMEM((256, 1024), jnp.bfloat16),
        ],
        compiler_params=pltpu.CompilerParams(vmem_limit_bytes=32 * 1024 * 1024),
    )(at, whole, high, low, mine, other, factor_inverse)
    updated = updated.reshape(2, 256, 2, 4, 128).swapaxes(2, 3).reshape(2, 256, 4, 256)
    return updated, jnp.swapaxes(factor_panel, 1, 2)


def solution(mesh):
    fine = Mesh(mesh.devices.reshape(SIZES), AXES)
    specs = (P(None, ROW, None, COL), P(None, ROW, COL), P())
    return jax.shard_map(
        on_device, mesh=fine, in_specs=specs, out_specs=specs[:2], check_vma=False
    )
```

time: 305 us -> 62.5 us (0.20)
  the two profiles are of different devices: /device:TPU:1 before, /device:TPU:259 now
where the time goes in v1:
time: 62.5 us; the launch traced here: 62.2 us
  blocking collectives  25.5 us (41%)
  starting transfers between devices  22.9 us (37%)
  Pallas kernels  6.41 us (10%)
  waiting for transfers between devices  4.92 us (8%)
  local copies, waits for them, and re-layouts  1.72 us (3%)
  between operations  0.68 us (1%)
    all_to_all x2, blocking collectives, gather(): return lax.all_to_all(many, axes, 0, 0, tiled=True)  25.5 us
    ppermute x1, starting transfers between devices, on_device(): other = lax.ppermute(mine, 'core', [(0, 1), (1, 0)])  13.6 us
    ppermute x1, starting transfers between devices, on_device(): sent = lax.ppermute(quarter, AXES, to_columns())  4.96 us
    ppermute x1, waiting for transfers between devices, on_device(): sent = lax.ppermute(quarter, AXES, to_columns())  4.92 us
    pallas_call x1, Pallas kernels, on_device(): pl.pallas_call(update_kernel, grid=(2, 256 // rows), out_shape=jax.ShapeD...  4.82 us
    all_to_all x1, starting transfers between devices, gather(): return lax.all_to_all(many, axes, 0, 0, tiled=True)  4.26 us
    broadcast_in_dim x3, local copies, waits for them, and re-layouts, gather(): many = jnp.broadcast_to(block[None], (n,) + block.shape)  1.71 us
    pallas_call x1, Pallas kernels, on_device(): pl.pallas_call(own_kernel, out_shape=[jax.ShapeDtypeStruct((2, 256, 256),...  1.59 us
  transfers between devices with their start and end apart: 3, of which 1 were waited for; matrix products, arithmetic and copies ran while one was open for 0% of the time, Pallas kernels for 3%

profile of v1, /device:TPU:259, one launch (start us, length us, event | category | flops | bytes accessed | tf_op | source)
XLA Modules:
  0.0 62.2 jit_solution(365140159884430031)
XLA Ops:
  0.6 0.0 copy-start.1
  0.6 0.8 %broadcast_in_dim.6 = f32[4,2,16,256]{3,2,1,0:T(8,128)S(1)} broadcast(f32[2,16,256]{2,1,0:T(8,128)} %bitcast.21), dimensions={1,2,3} | broadcast | bytes 163840 | tf_op jit(solution)/shard_map/broadcast_in_dim | solution.py:39
  1.5 14.0 %all_to_all.15 = f32[4,2,16,256]{3,2,1,0:T(8,128)S(1)} all-to-all(f32[4,2,16,256]{3,2,1,0:T(8,128)S(1)} %broadcast_in_dim.6), channel_id=1, replica_groups=mesh['zg'=4,'z0'=2,'yl'=2,'core'=2,'x'=4,'yh'=4] {'yh'}, dimensions={0} | all-to-all | bytes 262144 | tf_op jit(solution)/shard_map/all_to_all | solution.py:40
  15.4 0.0 copy-start
  15.4 0.9 %broadcast_in_dim.7 = f32[4,4,2,16,256]{4,3,2,1,0:T(8,128)} broadcast(f32[4,2,16,256]{3,2,1,0:T(8,128)S(1)} %all_to_all.15), dimensions={1,2,3,4} | broadcast | bytes 655360 | tf_op jit(solution)/shard_map/broadcast_in_dim | solution.py:39
  16.3 4.3 %all-to-all-start.1 = ((f32[4,4,2,16,256]{4,3,2,1,0:T(8,128)}), f32[4,4,2,16,256]{4,3,2,1,0:T(8,128)S(1)}, u32[]{:S(2)}, u32[]{:S(2)}) async-start(f32[4,4,2,16,256]{4,3,2,1,0:T(8,128)} %broadcast_in_dim.7), calls=%async_computation.1 | async-start | bytes 1048576 | tf_op jit(solution)/shard_map/all_to_all | solution.py:40
  20.5 5.0 %collective-permute-start = (f32[4,2,16,256]{3,2,1,0:T(8,128)S(1)}, f32[4,2,16,256]{3,2,1,0:T(8,128)S(1)}, u32[]{:S(2)}, u32[]{:S(2)}) collective-permute-start(f32[4,2,16,256]{3,2,1,0:T(8,128)S(1)} %all_to_all.15), channel_id=1, source_target_pairs={{0,0},{1,128},{2,256},{3,384},{4,160},{5,288},{6,416},{7,32},{8,32... | collective-permute-start | bytes 393224 | tf_op jit(solution)/shard_map/ppermute | solution.py:90
  25.5 4.9 %collective-permute-done = f32[4,2,16,256]{3,2,1,0:T(8,128)S(1)} collective-permute-done((f32[4,2,16,256]{3,2,1,0:T(8,128)S(1)}, f32[4,2,16,256]{3,2,1,0:T(8,128)S(1)}, u32[]{:S(2)}, u32[]{:S(2)}) %collective-permute-start) | collective-permute-done | bytes 131104 | tf_op jit(solution)/shard_map/ppermute | solution.py:90
  30.4 0.0 all-to-all-done.1
  30.4 0.1 broadcast_in_dim.8
  30.5 11.5 %all_to_all.16 = f32[4,4,2,16,256]{4,3,2,1,0:T(8,128)S(1)} all-to-all(f32[4,4,2,16,256]{4,3,2,1,0:T(8,128)S(1)} %broadcast_in_dim.8), channel_id=1, replica_groups=mesh['zg'=4,'z0'=2,'yl'=2,'core'=2,'x'=4,'yh'=4] {'z0','yl'}, dimensions={0} | all-to-all | bytes 1048576 | tf_op jit(solution)/shard_map/all_to_all | solution.py:40
  42.0 13.6 %collective-permute-start.1 = (f32[16,2,16,256]{3,2,1,0:T(8,128)S(1)}, f32[16,2,16,256]{3,2,1,0:T(8,128)}, u32[]{:S(2)}, u32[]{:S(2)}) collective-permute-start(f32[16,2,16,256]{3,2,1,0:T(8,128)S(1)} %bitcast.17), channel_id=1, source_target_pairs={{0,16},{16,0},{1,17},{17,1},{2,18},{18,2},{3,19},{19,3},{4,20},{20... | collective-permute-start | bytes 1572872 | tf_op jit(solution)/shard_map/ppermute | solution.py:95
  55.7 0.1 pad_add_fusion.at_ref
  55.7 0.0 copy-done.1
  55.7 1.6 %shard_map.50 = (bf16[2,256,256]{2,1,0:T(8,128)(2,1)S(1)}, bf16[2,256,256]{2,1,0:T(8,128)(2,1)S(1)}, f32[2,16,256]{2,1,0:T(8,128)}) custom-call(s32[2]{0:T(128)S(1)} %pad_add_fusion.at_ref, f32[16,2,16,256]{3,2,1,0:T(8,128)S(1)} %bitcast.19, f32[256,256]{1,0:T(8,128)S(1)} %copy-done.1), custom_call_target="tpu_custom_call" | custom-call | tf_op jit(solution)/shard_map/pallas_call | solution.py:99
  57.3 0.0 collective-permute-done.1.other_ref
  57.3 0.0 copy-done
  57.3 4.8 %shard_map.51 = f32[2,256,8,128]{3,2,1,0:T(8,128)} custom-call(s32[2]{0:T(128)S(1)} %pad_add_fusion.at_ref, f32[2,256,8,128]{3,2,1,0:T(8,128)S(1)} %bitcast.16, bf16[2,256,256]{2,1,0:T(8,128)(2,1)S(1)} %get-tuple-element.8.high_ref, bf16[2,256,256]{2,1,0:T(8,128)(2,1)S(1)} %get-tuple-element.9.low_ref, f32[16,2,16,256]{3,2,1,0:T(8,128)S(1)} %bitcast.18, ...), custom_call_target="tpu_custom_call" | custom-call | tf_op jit(solution)/shard_map/pallas_call | solution.py:113
Async XLA Ops:
  0.6 55.1 %copy-start.1 = (f32[256,256]{1,0:T(8,128)S(1)}, f32[256,256]{1,0:T(8,128)}, u32[]{:S(2)}) copy-start(f32[256,256]{1,0:T(8,128)} %inverse_ref.3) | copy-start | bytes 786436
  15.4 41.9 %copy-start = (f32[2,256,4,256]{3,2,1,0:T(4,128)S(1)}, f32[2,256,4,256]{3,2,1,0:T(4,128)}, u32[]{:S(2)}) copy-start(f32[2,256,4,256]{3,2,1,0:T(4,128)} %param.3) | copy-start | bytes 6291460
  16.3 14.2 %all-to-all-start.1 = ((f32[4,4,2,16,256]{4,3,2,1,0:T(8,128)}), f32[4,4,2,16,256]{4,3,2,1,0:T(8,128)S(1)}, u32[]{:S(2)}, u32[]{:S(2)}) async-start(f32[4,4,2,16,256]{4,3,2,1,0:T(8,128)} %broadcast_in_dim.7), calls=%async_computation.1 | async-start | bytes 1048576 | tf_op jit(solution)/shard_map/all_to_all | solution.py:40
  20.5 9.9 %collective-permute-start = (f32[4,2,16,256]{3,2,1,0:T(8,128)S(1)}, f32[4,2,16,256]{3,2,1,0:T(8,128)S(1)}, u32[]{:S(2)}, u32[]{:S(2)}) collective-permute-start(f32[4,2,16,256]{3,2,1,0:T(8,128)S(1)} %all_to_all.15), channel_id=1, source_target_pairs={{0,0},{1,128},{2,256},{3,384},{4,160},{5,288},{6,416},{7,32},{8,32... | collective-permute-start | bytes 393224 | tf_op jit(solution)/shard_map/ppermute | solution.py:90
  42.0 15.3 %collective-permute-start.1 = (f32[16,2,16,256]{3,2,1,0:T(8,128)S(1)}, f32[16,2,16,256]{3,2,1,0:T(8,128)}, u32[]{:S(2)}, u32[]{:S(2)}) collective-permute-start(f32[16,2,16,256]{3,2,1,0:T(8,128)S(1)} %bitcast.17), channel_id=1, source_target_pairs={{0,16},{16,0},{1,17},{17,1},{2,18},{18,2},{3,19},{19,3},{4,20},{20... | collective-permute-start | bytes 1572872 | tf_op jit(solution)/shard_map/ppermute | solution.py:95

commit v2 on v1

v2 whole, which is shorter than its diff:
```python
import functools

import jax
import jax.numpy as jnp
from jax import lax
from jax.experimental import pallas as pl
from jax.experimental.pallas import tpu as pltpu
from jax.sharding import Mesh
from jax.sharding import PartitionSpec as P

AXES = ("z", "yl", "core", "x", "yh")
SIZES = (8, 2, 2, 4, 4)
ROW, COL = AXES[:3], AXES[3:]
ROWS = 128


def to_columns():
    pairs = []
    for p in range(32):
        for q in range(16):
            pairs.append((p * 16 + q, (q * 2 + p // 16) * 16 + p % 16))
    return pairs


def split(value):
    high = value.astype(jnp.bfloat16)
    low = (value - high.astype(jnp.float32)).astype(jnp.bfloat16)
    return high, low


def product(left, right):
    dot = functools.partial(jnp.dot, preferred_element_type=jnp.float32)
    return dot(left[0], right[0]) + (dot(left[0], right[1]) + dot(left[1], right[0]))


def own_kernel(at_ref, rows_ref, inverse_ref, high_ref, low_ref, panel_ref):
    inverse = split(inverse_ref[...])
    start = pl.multiple_of(at_ref[0] * 16, 16)
    for t in range(2):
        factor = product(inverse, split(rows_ref[:, t].reshape(256, 256)))
        high_ref[t], low_ref[t] = split(factor.T)
        panel_ref[t] = product(
            split(inverse_ref[pl.ds(start, 16), :]), split(rows_ref[:, t].reshape(256, 256))
        )


def update_kernel(at_ref, trailing_ref, high_ref, low_ref, mine_ref, other_ref, inverse_ref, out_ref, right_high, right_low, done, sems):
    inverse = split(inverse_ref[...])
    for ref, half in ((mine_ref, at_ref[1]), (other_ref, 1 - at_ref[1])):
        for t in range(2):
            high, low = split(product(inverse, split(ref[:, t].reshape(256, 256))))
            for part in range(2):
                start = pl.multiple_of((part * 4 + t * 2 + half) * 128, 128)
                right_high[:, pl.ds(start, 128)] = high[:, part * 128 : part * 128 + 128]
                right_low[:, pl.ds(start, 128)] = low[:, part * 128 : part * 128 + 128]
    right = (right_high[...], right_low[...])
    copies = []
    for t in range(2):
        for i in range(256 // ROWS):
            rows = pl.ds(i * ROWS, ROWS)
            total = product((high_ref[t, rows], low_ref[t, rows]), right)
            done[t, rows] = trailing_ref[t, rows] - total.reshape(ROWS, 8, 128)
            copy = pltpu.make_async_copy(done.at[t, rows], out_ref.at[t, rows], sems.at[len(copies)])
            copy.start()
            copies.append(copy)
    for copy in copies:
        copy.wait()


def on_device(trailing, panel, factor_inverse):
    col = lax.axis_index(COL)
    core = lax.axis_index("core")
    at = jnp.stack([col, core]).astype(jnp.int32)
    sliver = jnp.swapaxes(panel, 1, 2)
    sent = lax.ppermute(sliver, AXES, to_columns())
    quarter = lax.all_gather(sliver, "yh")
    sent, quarter = lax.optimization_barrier((sent, quarter))
    many = jnp.broadcast_to(sent[None], (16, 2, 16, 256))
    mine = lax.all_to_all(many, ("z", "yl"), 0, 0, tiled=True)
    own = lax.all_gather(quarter, "x").reshape(16, 2, 16, 256)
    mine, own = lax.optimization_barrier((mine, own))
    other = lax.ppermute(mine, "core", [(0, 1), (1, 0)])

    smem = pl.BlockSpec(memory_space=pltpu.SMEM)
    vmem = pl.BlockSpec(memory_space=pltpu.VMEM)
    high, low, factor_panel = pl.pallas_call(
        own_kernel,
        out_shape=[
            jax.ShapeDtypeStruct((2, 256, 256), jnp.bfloat16),
            jax.ShapeDtypeStruct((2, 256, 256), jnp.bfloat16),
            jax.ShapeDtypeStruct((2, 16, 256), jnp.float32),
        ],
        in_specs=[smem, vmem, vmem],
        out_specs=[vmem, vmem, vmem],
        compiler_params=pltpu.CompilerParams(vmem_limit_bytes=32 * 1024 * 1024),
    )(at, own, factor_inverse)

    whole = trailing.reshape(2, 256, 4, 2, 128).swapaxes(2, 3).reshape(2, 256, 8, 128)
    updated = pl.pallas_call(
        update_kernel,
        out_shape=jax.ShapeDtypeStruct((2, 256, 8, 128), jnp.float32),
        in_specs=[smem] + [vmem] * 6,
        out_specs=pl.BlockSpec(memory_space=pl.ANY),
        scratch_shapes=[
            pltpu.VMEM((256, 1024), jnp.bfloat16),
            pltpu.VMEM((256, 1024), jnp.bfloat16),
            pltpu.VMEM((2, 256, 8, 128), jnp.float32),
            pltpu.SemaphoreType.DMA((512 // ROWS,)),
        ],
        compiler_params=pltpu.CompilerParams(vmem_limit_bytes=32 * 1024 * 1024),
    )(at, whole, high, low, mine, other, factor_inverse)
    updated = updated.reshape(2, 256, 2, 4, 128).swapaxes(2, 3).reshape(2, 256, 4, 256)
    return updated, jnp.swapaxes(factor_panel, 1, 2)


def solution(mesh):
    fine = Mesh(mesh.devices.reshape(SIZES), AXES)
    specs = (P(None, ROW, None, COL), P(None, ROW, COL), P())
    return jax.shard_map(
        on_device, mesh=fine, in_specs=specs, out_specs=specs[:2], check_vma=False
    )
```

time: 62.5 us -> 57.8 us (0.925)
  the two profiles are of different devices: /device:TPU:259 before, /device:TPU:1 now
where the time goes in v2:
time: 57.8 us; the launch traced here: 57.4 us
  blocking collectives  27.8 us (48%)
  starting transfers between devices  22.1 us (38%)
  Pallas kernels  5.43 us (9%)
  local copies, waits for them, and re-layouts  0.86 us (1%)
  between operations  0.68 us (1%)
    all_gather x1, blocking collectives, on_device(): own = lax.all_gather(quarter, 'x').reshape(16, 2, 16, 256)  14.7 us
    all_gather x1, blocking collectives, on_device(): quarter = lax.all_gather(sliver, 'yh')  13.1 us
    all_to_all x1, starting transfers between devices, on_device(): mine = lax.all_to_all(many, ('z', 'yl'), 0, 0, tiled=True)  8.52 us
    ppermute x1, starting transfers between devices, on_device(): other = lax.ppermute(mine, 'core', [(0, 1), (1, 0)])  7.87 us
    ppermute x1, starting transfers between devices, on_device(): sent = lax.ppermute(sliver, AXES, to_columns())  5.74 us
    pallas_call x1, Pallas kernels, on_device(): pl.pallas_call(update_kernel, out_shape=jax.ShapeDtypeStruct((2, 256, 8,...  3.84 us
    pallas_call x1, Pallas kernels, on_device(): pl.pallas_call(own_kernel, out_shape=[jax.ShapeDtypeStruct((2, 256, 256),...  1.59 us
  transfers between devices with their start and end apart: 3, of which 1 were waited for; matrix products, arithmetic and copies ran while one was open for 0% of the time, Pallas kernels for 3%

profile of v2, /device:TPU:1, one launch (start us, length us, event | category | flops | bytes accessed | tf_op | source)
XLA Modules:
  0.0 57.4 jit_solution(2839097635819784438)
XLA Ops:
  0.6 0.0 copy-start.1
  0.6 0.0 copy-start
  0.6 5.7 %collective-permute-start = (f32[2,16,256]{2,1,0:T(8,128)}, f32[2,16,256]{2,1,0:T(8,128)S(1)}, u32[]{:S(2)}, u32[]{:S(2)}) collective-permute-start(f32[2,16,256]{2,1,0:T(8,128)} %bitcast.18), channel_id=1, source_target_pairs={{0,0},{1,32},{2,64},{3,96},{4,128},{5,160},{6,192},{7,224},{8,256}... | collective-permute-start | bytes 98312 | tf_op jit(solution)/shard_map/ppermute | solution.py:75
  6.4 13.1 %all-gather = f32[8,16,256]{2,1,0:T(8,128)S(1)} all-gather(f32[2,16,256]{2,1,0:T(8,128)} %bitcast.19), channel_id=2, replica_groups=mesh['z'=8,'yl'=2,'core'=2,'x'=4,'yh'=4] {'yh'}, dimensions={0}, use_global_device_ids=true | all-gather | bytes 163840 | tf_op jit(solution)/shard_map/all_gather | solution.py:76
  19.5 0.0 collective-permute-done
  19.5 0.9 %broadcast_in_dim.2 = f32[16,2,16,256]{3,2,1,0:T(8,128)} broadcast(f32[2,16,256]{2,1,0:T(8,128)S(1)} %collective-permute-done), dimensions={1,2,3} | broadcast | bytes 557056 | tf_op jit(solution)/shard_map/broadcast_in_dim | solution.py:78
  20.4 8.5 %all-to-all-start = ((f32[16,2,16,256]{3,2,1,0:T(8,128)}), f32[16,2,16,256]{3,2,1,0:T(8,128)S(1)}, u32[]{:S(2)}, u32[]{:S(2)}) async-start(f32[16,2,16,256]{3,2,1,0:T(8,128)} %broadcast_in_dim.2), calls=%async_computation | async-start | bytes 1048576 | tf_op jit(solution)/shard_map/all_to_all | solution.py:79
  28.9 14.7 %all-gather.1.rows_ref = f32[16,2,16,256]{3,2,1,0:T(8,128)S(1)} all-gather(f32[4,2,16,256]{3,2,1,0:T(8,128)S(1)} %bitcast.17), channel_id=3, replica_groups=mesh['z'=8,'yl'=2,'core'=2,'x'=4,'yh'=4] {'x'}, dimensions={0}, use_global_device_ids=true | all-gather | bytes 655360 | tf_op jit(solution)/shard_map/all_gather | solution.py:80
  43.6 0.4 all-to-all-done.mine_ref
  44.0 7.9 %collective-permute-start.1 = (f32[16,2,16,256]{3,2,1,0:T(8,128)S(1)}, f32[16,2,16,256]{3,2,1,0:T(8,128)}, u32[]{:S(2)}, u32[]{:S(2)}) collective-permute-start(f32[16,2,16,256]{3,2,1,0:T(8,128)S(1)} %all-to-all-done.mine_ref), channel_id=1, source_target_pairs={{0,16},{16,0},{1,17},{17,1},{2,18},{18,2},{3,19},{19,3},{4,20},{20... | collective-permute-start | bytes 1572872 | tf_op jit(solution)/shard_map/ppermute | solution.py:82
  51.9 0.1 pad_add_fusion.at_ref
  51.9 0.0 copy-done.1
  52.0 1.6 %shard_map.50 = (bf16[2,256,256]{2,1,0:T(8,128)(2,1)S(1)}, bf16[2,256,256]{2,1,0:T(8,128)(2,1)S(1)}, f32[2,16,256]{2,1,0:T(8,128)}) custom-call(s32[2]{0:T(128)S(1)} %pad_add_fusion.at_ref, f32[16,2,16,256]{3,2,1,0:T(8,128)S(1)} %all-gather.1.rows_ref, f32[256,256]{1,0:T(8,128)S(1)} %copy-done.1), custom_call_target="tpu_custom_call" | custom-call | tf_op jit(solution)/shard_map/pallas_call | solution.py:86
  53.5 0.0 collective-permute-done.1.other_ref
  53.5 0.0 copy-done
  53.5 3.8 %shard_map.51 = f32[2,256,8,128]{3,2,1,0:T(8,128)} custom-call(s32[2]{0:T(128)S(1)} %pad_add_fusion.at_ref, f32[2,256,8,128]{3,2,1,0:T(8,128)S(1)} %bitcast.15, bf16[2,256,256]{2,1,0:T(8,128)(2,1)S(1)} %get-tuple-element.12.high_ref, bf16[2,256,256]{2,1,0:T(8,128)(2,1)S(1)} %get-tuple-element.13.low_ref, f32[16,2,16,256]{3,2,1,0:T(8,128)S(1)} %all-to-all-done.mine_ref, ...), custom_call_target="tpu_custom_call" | custom-call | tf_op jit(solution)/shard_map/pallas_call | solution.py:99
Async XLA Ops:
  0.6 51.3 %copy-start.1 = (f32[256,256]{1,0:T(8,128)S(1)}, f32[256,256]{1,0:T(8,128)}, u32[]{:S(2)}) copy-start(f32[256,256]{1,0:T(8,128)} %inverse_ref.3) | copy-start | bytes 786436
  0.6 52.9 %copy-start = (f32[2,256,4,256]{3,2,1,0:T(4,128)S(1)}, f32[2,256,4,256]{3,2,1,0:T(4,128)}, u32[]{:S(2)}) copy-start(f32[2,256,4,256]{3,2,1,0:T(4,128)} %param.3) | copy-start | bytes 6291460
  0.6 18.9 %collective-permute-start = (f32[2,16,256]{2,1,0:T(8,128)}, f32[2,16,256]{2,1,0:T(8,128)S(1)}, u32[]{:S(2)}, u32[]{:S(2)}) collective-permute-start(f32[2,16,256]{2,1,0:T(8,128)} %bitcast.18), channel_id=1, source_target_pairs={{0,0},{1,32},{2,64},{3,96},{4,128},{5,160},{6,192},{7,224},{8,256}... | collective-permute-start | bytes 98312 | tf_op jit(solution)/shard_map/ppermute | solution.py:75
  20.4 23.6 %all-to-all-start = ((f32[16,2,16,256]{3,2,1,0:T(8,128)}), f32[16,2,16,256]{3,2,1,0:T(8,128)S(1)}, u32[]{:S(2)}, u32[]{:S(2)}) async-start(f32[16,2,16,256]{3,2,1,0:T(8,128)} %broadcast_in_dim.2), calls=%async_computation | async-start | bytes 1048576 | tf_op jit(solution)/shard_map/all_to_all | solution.py:79
  44.0 9.6 %collective-permute-start.1 = (f32[16,2,16,256]{3,2,1,0:T(8,128)S(1)}, f32[16,2,16,256]{3,2,1,0:T(8,128)}, u32[]{:S(2)}, u32[]{:S(2)}) collective-permute-start(f32[16,2,16,256]{3,2,1,0:T(8,128)S(1)} %all-to-all-done.mine_ref), channel_id=1, source_target_pairs={{0,16},{16,0},{1,17},{17,1},{2,18},{18,2},{3,19},{19,3},{4,20},{20... | collective-permute-start | bytes 1572872 | tf_op jit(solution)/shard_map/ppermute | solution.py:82

commit v3 on v2

--- a/solution.py
+++ b/solution.py
@@ -20,6 +20,11 @@
         for q in range(16):
             pairs.append((p * 16 + q, (q * 2 + p // 16) * 16 + p % 16))
     return pairs
+
+
+def gather_pairs(block, axis):
+    block = lax.all_gather(block, axis, axis=0, tiled=True, axis_index_groups=[[0, 1], [2, 3]])
+    return lax.all_gather(block, axis, axis=0, tiled=True, axis_index_groups=[[0, 3], [1, 2]])
 
 
 def split(value):
@@ -73,11 +78,11 @@
     at = jnp.stack([col, core]).astype(jnp.int32)
     sliver = jnp.swapaxes(panel, 1, 2)
     sent = lax.ppermute(sliver, AXES, to_columns())
-    quarter = lax.all_gather(sliver, "yh")
+    quarter = gather_pairs(sliver[None], "yh")
     sent, quarter = lax.optimization_barrier((sent, quarter))
     many = jnp.broadcast_to(sent[None], (16, 2, 16, 256))
     mine = lax.all_to_all(many, ("z", "yl"), 0, 0, tiled=True)
-    own = lax.all_gather(quarter, "x").reshape(16, 2, 16, 256)
+    own = lax.all_gather(quarter, "x", axis=0, tiled=True)
     mine, own = lax.optimization_barrier((mine, own))
     other = lax.ppermute(mine, "core", [(0, 1), (1, 0)])
 

time: 57.8 us -> 57.4 us (level)
  starting transfers between devices: 22.1 us -> 21.5 us
    all_gather x2 -> x3, blocking collectives: 27.8 us -> 27.9 us  [the longest x1 15.6 us: on_device(): own = lax.all_gather(quarter, 'x', axis=0, tiled=True)]
  transfers between devices with their start and end apart: 3 -> 3, of which waited for: 1 -> 0; matrix products, arithmetic and copies ran while one was open for 0% -> 0% of each run, Pallas kernels for 3% -> 3%
where the time goes in v3:
time: 57.4 us; the launch traced here: 56.4 us
  blocking collectives  27.9 us (49%)
  starting transfers between devices  21.5 us (37%)
  Pallas kernels  5.43 us (9%)
  local copies, waits for them, and re-layouts  0.86 us (1%)
  between operations  0.68 us (1%)
    all_gather x1, blocking collectives, on_device(): own = lax.all_gather(quarter, 'x', axis=0, tiled=True)  15.6 us
    all_to_all x1, starting transfers between devices, on_device(): mine = lax.all_to_all(many, ('z', 'yl'), 0, 0, tiled=True)  8.04 us
    ppermute x1, starting transfers between devices, on_device(): other = lax.ppermute(mine, 'core', [(0, 1), (1, 0)])  7.7 us
    all_gather x1, blocking collectives, gather_pairs(): lax.all_gather(block, axis, axis=0, tiled=True, axis_index_groups=[[0, 3]...  7.62 us
    ppermute x1, starting transfers between devices, on_device(): sent = lax.ppermute(sliver, AXES, to_columns())  5.74 us
    all_gather x1, blocking collectives, gather_pairs(): lax.all_gather(block, axis, axis=0, tiled=True, axis_index_groups=[[0, 1]...  4.65 us
    pallas_call x1, Pallas kernels, on_device(): pl.pallas_call(update_kernel, out_shape=jax.ShapeDtypeStruct((2, 256, 8,...  3.84 us
    pallas_call x1, Pallas kernels, on_device(): pl.pallas_call(own_kernel, out_shape=[jax.ShapeDtypeStruct((2, 256, 256),...  1.59 us
  transfers between devices with their start and end apart: 3, of which 0 were waited for; matrix products, arithmetic and copies ran while one was open for 0% of the time, Pallas kernels for 3%

profile of v3, /device:TPU:1, one launch (start us, length us, event | category | flops | bytes accessed | tf_op | source)
XLA Modules:
  0.0 56.4 jit_solution(9882904944570423511)
XLA Ops:
  0.6 0.0 copy-start.1
  0.6 0.0 copy-start
  0.6 5.7 %collective-permute-start = (f32[2,16,256]{2,1,0:T(8,128)}, f32[2,16,256]{2,1,0:T(8,128)S(1)}, u32[]{:S(2)}, u32[]{:S(2)}) collective-permute-start(f32[2,16,256]{2,1,0:T(8,128)} %bitcast.18), channel_id=1, source_target_pairs={{0,0},{1,32},{2,64},{3,96},{4,128},{5,160},{6,192},{7,224},{8,256}... | collective-permute-start | bytes 98312 | tf_op jit(solution)/shard_map/ppermute | solution.py:80
  6.4 4.7 %all-gather = f32[4,16,256]{2,1,0:T(8,128)S(1)} all-gather(f32[2,16,256]{2,1,0:T(8,128)} %bitcast.19), channel_id=2, replica_groups={{0,1},{2,3},{4,5},{6,7},{8,9},{10,11},{12,13},{14,15},{16,17},{18,19},{..., dimensions={0}, use_global_device_ids=true | all-gather | bytes 98304 | tf_op jit(solution)/shard_map/all_gather | solution.py:26
  11.1 7.6 %all_gather.10 = f32[4,2,16,256]{3,2,1,0:T(8,128)S(1)} all-gather(f32[2,2,16,256]{3,2,1,0:T(8,128)S(1)} %bitcast.17), channel_id=1, replica_groups={{0,3},{1,2},{4,7},{5,6},{8,11},{9,10},{12,15},{13,14},{16,19},{17,18},{..., dimensions={0}, use_global_device_ids=true | all-gather | bytes 196608 | tf_op jit(solution)/shard_map/all_gather | solution.py:27
  18.7 0.0 collective-permute-done
  18.7 0.9 %broadcast_in_dim.10 = f32[16,2,16,256]{3,2,1,0:T(8,128)} broadcast(f32[2,16,256]{2,1,0:T(8,128)S(1)} %collective-permute-done), dimensions={1,2,3} | broadcast | bytes 557056 | tf_op jit(solution)/shard_map/broadcast_in_dim | solution.py:83
  19.5 8.0 %all-to-all-start = ((f32[16,2,16,256]{3,2,1,0:T(8,128)}), f32[16,2,16,256]{3,2,1,0:T(8,128)S(1)}, u32[]{:S(2)}, u32[]{:S(2)}) async-start(f32[16,2,16,256]{3,2,1,0:T(8,128)} %broadcast_in_dim.10), calls=%async_computation | async-start | bytes 1048576 | tf_op jit(solution)/shard_map/all_to_all | solution.py:84
  27.6 15.6 %all_gather.11.rows_ref = f32[16,2,16,256]{3,2,1,0:T(8,128)S(1)} all-gather(f32[4,2,16,256]{3,2,1,0:T(8,128)S(1)} %all_gather.10), channel_id=1, replica_groups=mesh['z'=8,'yl'=2,'core'=2,'x'=4,'yh'=4] {'x'}, dimensions={0}, use_global_device_ids=true | all-gather | bytes 655360 | tf_op jit(solution)/shard_map/all_gather | solution.py:85
  43.2 0.0 all-to-all-done.mine_ref
  43.2 7.7 %collective-permute-start.1 = (f32[16,2,16,256]{3,2,1,0:T(8,128)S(1)}, f32[16,2,16,256]{3,2,1,0:T(8,128)}, u32[]{:S(2)}, u32[]{:S(2)}) collective-permute-start(f32[16,2,16,256]{3,2,1,0:T(8,128)S(1)} %all-to-all-done.mine_ref), channel_id=1, source_target_pairs={{0,16},{16,0},{1,17},{17,1},{2,18},{18,2},{3,19},{19,3},{4,20},{20... | collective-permute-start | bytes 1572872 | tf_op jit(solution)/shard_map/ppermute | solution.py:87
  50.9 0.1 pad_add_fusion.at_ref
  51.0 0.0 copy-done.1
  51.0 1.6 %shard_map.50 = (bf16[2,256,256]{2,1,0:T(8,128)(2,1)S(1)}, bf16[2,256,256]{2,1,0:T(8,128)(2,1)S(1)}, f32[2,16,256]{2,1,0:T(8,128)}) custom-call(s32[2]{0:T(128)S(1)} %pad_add_fusion.at_ref, f32[16,2,16,256]{3,2,1,0:T(8,128)S(1)} %all_gather.11.rows_ref, f32[256,256]{1,0:T(8,128)S(1)} %copy-done.1), custom_call_target="tpu_custom_call" | custom-call | tf_op jit(solution)/shard_map/pallas_call | solution.py:91
  52.6 0.0 collective-permute-done.1.other_ref
  52.6 0.0 copy-done
  52.6 3.8 %shard_map.51 = f32[2,256,8,128]{3,2,1,0:T(8,128)} custom-call(s32[2]{0:T(128)S(1)} %pad_add_fusion.at_ref, f32[2,256,8,128]{3,2,1,0:T(8,128)S(1)} %bitcast.15, bf16[2,256,256]{2,1,0:T(8,128)(2,1)S(1)} %get-tuple-element.12.high_ref, bf16[2,256,256]{2,1,0:T(8,128)(2,1)S(1)} %get-tuple-element.13.low_ref, f32[16,2,16,256]{3,2,1,0:T(8,128)S(1)} %all-to-all-done.mine_ref, ...), custom_call_target="tpu_custom_call" | custom-call | tf_op jit(solution)/shard_map/pallas_call | solution.py:104
Async XLA Ops:
  0.6 50.4 %copy-start.1 = (f32[256,256]{1,0:T(8,128)S(1)}, f32[256,256]{1,0:T(8,128)}, u32[]{:S(2)}) copy-start(f32[256,256]{1,0:T(8,128)} %inverse_ref.3) | copy-start | bytes 786436
  0.6 52.0 %copy-start = (f32[2,256,4,256]{3,2,1,0:T(4,128)S(1)}, f32[2,256,4,256]{3,2,1,0:T(4,128)}, u32[]{:S(2)}) copy-start(f32[2,256,4,256]{3,2,1,0:T(4,128)} %param.3) | copy-start | bytes 6291460
  0.6 18.0 %collective-permute-start = (f32[2,16,256]{2,1,0:T(8,128)}, f32[2,16,256]{2,1,0:T(8,128)S(1)}, u32[]{:S(2)}, u32[]{:S(2)}) collective-permute-start(f32[2,16,256]{2,1,0:T(8,128)} %bitcast.18), channel_id=1, source_target_pairs={{0,0},{1,32},{2,64},{3,96},{4,128},{5,160},{6,192},{7,224},{8,256}... | collective-permute-start | bytes 98312 | tf_op jit(solution)/shard_map/ppermute | solution.py:80
  19.5 23.7 %all-to-all-start = ((f32[16,2,16,256]{3,2,1,0:T(8,128)}), f32[16,2,16,256]{3,2,1,0:T(8,128)S(1)}, u32[]{:S(2)}, u32[]{:S(2)}) async-start(f32[16,2,16,256]{3,2,1,0:T(8,128)} %broadcast_in_dim.10), calls=%async_computation | async-start | bytes 1048576 | tf_op jit(solution)/shard_map/all_to_all | solution.py:84
  43.2 9.4 %collective-permute-start.1 = (f32[16,2,16,256]{3,2,1,0:T(8,128)S(1)}, f32[16,2,16,256]{3,2,1,0:T(8,128)}, u32[]{:S(2)}, u32[]{:S(2)}) collective-permute-start(f32[16,2,16,256]{3,2,1,0:T(8,128)S(1)} %all-to-all-done.mine_ref), channel_id=1, source_target_pairs={{0,16},{16,0},{1,17},{17,1},{2,18},{18,2},{3,19},{19,3},{4,20},{20... | collective-permute-start | bytes 1572872 | tf_op jit(solution)/shard_map/ppermute | solution.py:87

commit v4 on v3

--- a/solution.py
+++ b/solution.py
@@ -38,36 +38,40 @@
     return dot(left[0], right[0]) + (dot(left[0], right[1]) + dot(left[1], right[0]))
 
 
-def own_kernel(at_ref, rows_ref, inverse_ref, high_ref, low_ref, panel_ref):
+def own_kernel(at_ref, rows_ref, mine_ref, inverse_ref, high_ref, low_ref, right_high_ref, right_low_ref, panel_ref):
     inverse = split(inverse_ref[...])
     start = pl.multiple_of(at_ref[0] * 16, 16)
     for t in range(2):
-        factor = product(inverse, split(rows_ref[:, t].reshape(256, 256)))
-        high_ref[t], low_ref[t] = split(factor.T)
-        panel_ref[t] = product(
-            split(inverse_ref[pl.ds(start, 16), :]), split(rows_ref[:, t].reshape(256, 256))
-        )
+        rows = split(rows_ref[:, t].reshape(256, 256))
+        high_ref[t], low_ref[t] = split(product(inverse, rows).T)
+        panel_ref[t] = product(split(inverse_ref[pl.ds(start, 16), :]), rows)
+    for t in range(2):
+        right_high_ref[t], right_low_ref[t] = split(product(inverse, split(mine_ref[:, t].reshape(256, 256))))
 
 
-def update_kernel(at_ref, trailing_ref, high_ref, low_ref, mine_ref, other_ref, inverse_ref, out_ref, right_high, right_low, done, sems):
+def update_kernel(at_ref, trailing_ref, high_ref, low_ref, mine_high, mine_low, other_ref, inverse_ref, out_ref, right_high, right_low, done, sems):
+    def place(t, half, high, low):
+        for part in range(2):
+            start = pl.multiple_of((part * 4 + t * 2 + half) * 128, 128)
+            right_high[:, pl.ds(start, 128)] = high[:, part * 128 : part * 128 + 128]
+            right_low[:, pl.ds(start, 128)] = low[:, part * 128 : part * 128 + 128]
+
     inverse = split(inverse_ref[...])
-    for ref, half in ((mine_ref, at_ref[1]), (other_ref, 1 - at_ref[1])):
-        for t in range(2):
-            high, low = split(product(inverse, split(ref[:, t].reshape(256, 256))))
-            for part in range(2):
-                start = pl.multiple_of((part * 4 + t * 2 + half) * 128, 128)
-                right_high[:, pl.ds(start, 128)] = high[:, part * 128 : part * 128 + 128]
-                right_low[:, pl.ds(start, 128)] = low[:, part * 128 : part * 128 + 128]
+    for t in range(2):
+        place(t, at_ref[1], mine_high[t], mine_low[t])
+        place(t, 1 - at_ref[1], *split(product(inverse, split(other_ref[:, t].reshape(256, 256)))))
     right = (right_high[...], right_low[...])
     copies = []
     for t in range(2):
         for i in range(256 // ROWS):
             rows = pl.ds(i * ROWS, ROWS)
             total = product((high_ref[t, rows], low_ref[t, rows]), right)
-            done[t, rows] = trailing_ref[t, rows] - total.reshape(ROWS, 8, 128)
-            copy = pltpu.make_async_copy(done.at[t, rows], out_ref.at[t, rows], sems.at[len(copies)])
-            copy.start()
-            copies.append(copy)
+            for part in range(2):
+                rows = pl.ds(i * ROWS + part * 64, 64)
+                done[t, rows] = trailing_ref[t, rows] - total[part * 64 : part * 64 + 64].reshape(64, 8, 128)
+                copy = pltpu.make_async_copy(done.at[t, rows], out_ref.at[t, rows], sems.at[len(copies)])
+                copy.start()
+                copies.append(copy)
     for copy in copies:
         copy.wait()
 
@@ -88,32 +92,29 @@
 
     smem = pl.BlockSpec(memory_space=pltpu.SMEM)
     vmem = pl.BlockSpec(memory_space=pltpu.VMEM)
-    high, low, factor_panel = pl.pallas_call(
+    square = jax.ShapeDtypeStruct((2, 256, 256), jnp.bfloat16)
+    high, low, right_high, right_low, factor_panel = pl.pallas_call(
         own_kernel,
-        out_shape=[
-            jax.ShapeDtypeStruct((2, 256, 256), jnp.bfloat16),
-            jax.ShapeDtypeStruct((2, 256, 256), jnp.bfloat16),
-            jax.ShapeDtypeStruct((2, 16, 256), jnp.float32),
-        ],
-        in_specs=[smem, vmem, vmem],
-        out_specs=[vmem, vmem, vmem],
+        out_shape=[square] * 4 + [jax.ShapeDtypeStruct((2, 16, 256), jnp.float32)],
+        in_specs=[smem, vmem, vmem, vmem],
+        out_specs=[vmem] * 5,
         compiler_params=pltpu.CompilerParams(vmem_limit_bytes=32 * 1024 * 1024),
-    )(at, own, factor_inverse)
+    )(at, own, mine, factor_inverse)
 
     whole = trailing.reshape(2, 256, 4, 2, 128).swapaxes(2, 3).reshape(2, 256, 8, 128)
     updated = pl.pallas_call(
         update_kernel,
         out_shape=jax.ShapeDtypeStruct((2, 256, 8, 128), jnp.float32),
-        in_specs=[smem] + [vmem] * 6,
+        in_specs=[smem] + [vmem] * 7,
         out_specs=pl.BlockSpec(memory_space=pl.ANY),
         scratch_shapes=[
             pltpu.VMEM((256, 1024), jnp.bfloat16),
             pltpu.VMEM((256, 1024), jnp.bfloat16),
             pltpu.VMEM((2, 256, 8, 128), jnp.float32),
-            pltpu.SemaphoreType.DMA((512 // ROWS,)),
+            pltpu.SemaphoreType.DMA((512 // 64,)),
         ],
         compiler_params=pltpu.CompilerParams(vmem_limit_bytes=32 * 1024 * 1024),
-    )(at, whole, high, low, mine, other, factor_inverse)
+    )(at, whole, high, low, right_high, right_low, other, factor_inverse)
     updated = updated.reshape(2, 256, 2, 4, 128).swapaxes(2, 3).reshape(2, 256, 4, 256)
     return updated, jnp.swapaxes(factor_panel, 1, 2)
 

time: 57.4 us -> 57.3 us (level)
  no operation moved by 1% of the time
where the time goes in v4:
time: 57.3 us; the launch traced here: 56.3 us
  blocking collectives  27.9 us (49%)
  starting transfers between devices  21.5 us (38%)
  Pallas kernels  5.31 us (9%)
  local copies, waits for them, and re-layouts  0.86 us (2%)
  between operations  0.68 us (1%)
    all_gather x1, blocking collectives, on_device(): own = lax.all_gather(quarter, 'x', axis=0, tiled=True)  15.6 us
    all_to_all x1, starting transfers between devices, on_device(): mine = lax.all_to_all(many, ('z', 'yl'), 0, 0, tiled=True)  8.04 us
    ppermute x1, starting transfers between devices, on_device(): other = lax.ppermute(mine, 'core', [(0, 1), (1, 0)])  7.7 us
    all_gather x1, blocking collectives, gather_pairs(): lax.all_gather(block, axis, axis=0, tiled=True, axis_index_groups=[[0, 3]...  7.62 us
    ppermute x1, starting transfers between devices, on_device(): sent = lax.ppermute(sliver, AXES, to_columns())  5.74 us
    all_gather x1, blocking collectives, gather_pairs(): lax.all_gather(block, axis, axis=0, tiled=True, axis_index_groups=[[0, 1]...  4.65 us
    pallas_call x1, Pallas kernels, on_device(): pl.pallas_call(update_kernel, out_shape=jax.ShapeDtypeStruct((2, 256, 8,...  3.59 us
    pallas_call x1, Pallas kernels, on_device(): pl.pallas_call(own_kernel, out_shape=[square] * 4 + [jax.ShapeDtypeStruct...  1.72 us
  transfers between devices with their start and end apart: 3, of which 0 were waited for; matrix products, arithmetic and copies ran while one was open for 0% of the time, Pallas kernels for 3%

profile of v4, /device:TPU:1, one launch (start us, length us, event | category | flops | bytes accessed | tf_op | source)
XLA Modules:
  0.0 56.3 jit_solution(4550699614193634067)
XLA Ops:
  0.6 0.0 copy-start.1
  0.6 0.0 copy-start
  0.6 5.7 %collective-permute-start = (f32[2,16,256]{2,1,0:T(8,128)}, f32[2,16,256]{2,1,0:T(8,128)S(1)}, u32[]{:S(2)}, u32[]{:S(2)}) collective-permute-start(f32[2,16,256]{2,1,0:T(8,128)} %bitcast.18), channel_id=1, source_target_pairs={{0,0},{1,32},{2,64},{3,96},{4,128},{5,160},{6,192},{7,224},{8,256}... | collective-permute-start | bytes 98312 | tf_op jit(solution)/shard_map/ppermute | solution.py:84
  6.4 4.7 %all-gather = f32[4,16,256]{2,1,0:T(8,128)S(1)} all-gather(f32[2,16,256]{2,1,0:T(8,128)} %bitcast.19), channel_id=2, replica_groups={{0,1},{2,3},{4,5},{6,7},{8,9},{10,11},{12,13},{14,15},{16,17},{18,19},{..., dimensions={0}, use_global_device_ids=true | all-gather | bytes 98304 | tf_op jit(solution)/shard_map/all_gather | solution.py:26
  11.1 7.6 %all_gather.10 = f32[4,2,16,256]{3,2,1,0:T(8,128)S(1)} all-gather(f32[2,2,16,256]{3,2,1,0:T(8,128)S(1)} %bitcast.17), channel_id=1, replica_groups={{0,3},{1,2},{4,7},{5,6},{8,11},{9,10},{12,15},{13,14},{16,19},{17,18},{..., dimensions={0}, use_global_device_ids=true | all-gather | bytes 196608 | tf_op jit(solution)/shard_map/all_gather | solution.py:27
  18.7 0.0 collective-permute-done
  18.7 0.9 %broadcast_in_dim.10 = f32[16,2,16,256]{3,2,1,0:T(8,128)} broadcast(f32[2,16,256]{2,1,0:T(8,128)S(1)} %collective-permute-done), dimensions={1,2,3} | broadcast | bytes 557056 | tf_op jit(solution)/shard_map/broadcast_in_dim | solution.py:87
  19.5 8.0 %all-to-all-start = ((f32[16,2,16,256]{3,2,1,0:T(8,128)}), f32[16,2,16,256]{3,2,1,0:T(8,128)S(1)}, u32[]{:S(2)}, u32[]{:S(2)}) async-start(f32[16,2,16,256]{3,2,1,0:T(8,128)} %broadcast_in_dim.10), calls=%async_computation | async-start | bytes 1048576 | tf_op jit(solution)/shard_map/all_to_all | solution.py:88
  27.6 15.6 %all_gather.11.rows_ref = f32[16,2,16,256]{3,2,1,0:T(8,128)S(1)} all-gather(f32[4,2,16,256]{3,2,1,0:T(8,128)S(1)} %all_gather.10), channel_id=1, replica_groups=mesh['z'=8,'yl'=2,'core'=2,'x'=4,'yh'=4] {'x'}, dimensions={0}, use_global_device_ids=true | all-gather | bytes 655360 | tf_op jit(solution)/shard_map/all_gather | solution.py:89
  43.2 0.0 all-to-all-done.mine_ref
  43.2 7.7 %collective-permute-start.1 = (f32[16,2,16,256]{3,2,1,0:T(8,128)S(1)}, f32[16,2,16,256]{3,2,1,0:T(8,128)}, u32[]{:S(2)}, u32[]{:S(2)}) collective-permute-start(f32[16,2,16,256]{3,2,1,0:T(8,128)S(1)} %all-to-all-done.mine_ref), channel_id=1, source_target_pairs={{0,16},{16,0},{1,17},{17,1},{2,18},{18,2},{3,19},{19,3},{4,20},{20... | collective-permute-start | bytes 1572872 | tf_op jit(solution)/shard_map/ppermute | solution.py:91
  50.9 0.1 pad_add_fusion.at_ref
  51.0 0.0 copy-done.1
  51.0 1.7 %shard_map.50 = (bf16[2,256,256]{2,1,0:T(8,128)(2,1)S(1)}, bf16[2,256,256]{2,1,0:T(8,128)(2,1)S(1)}, bf16[2,256,256]{2,1,0:T(8,128)(2,1)S(1)}, bf16[2,256,256]{2,1,0:T(8,128)(2,1)S(1)}, f32[2,16,256]{2,1,0:T(8,128)}) custom-call(s32[2]{0:T(128)S(1)} %pad_add_fusion.at_ref, f32[16,2,16,256]{3,2,1,0:T(8,128)S(1)} %all_gather.11.rows_ref, ...), custom_call_target="tpu_custom_call" | custom-call | tf_op jit(solution)/shard_map/pallas_call | solution.py:96
  52.7 0.0 collective-permute-done.1.other_ref
  52.7 0.0 copy-done
  52.7 3.6 %shard_map.51 = f32[2,256,8,128]{3,2,1,0:T(8,128)} custom-call(s32[2]{0:T(128)S(1)} %pad_add_fusion.at_ref, f32[2,256,8,128]{3,2,1,0:T(8,128)S(1)} %bitcast.15, bf16[2,256,256]{2,1,0:T(8,128)(2,1)S(1)} %get-tuple-element.15.high_ref, bf16[2,256,256]{2,1,0:T(8,128)(2,1)S(1)} %get-tuple-element.16.low_ref, ...), custom_call_target="tpu_custom_call" | custom-call | tf_op jit(solution)/shard_map/pallas_call | solution.py:105
Async XLA Ops:
  0.6 50.4 %copy-start.1 = (f32[256,256]{1,0:T(8,128)S(1)}, f32[256,256]{1,0:T(8,128)}, u32[]{:S(2)}) copy-start(f32[256,256]{1,0:T(8,128)} %inverse_ref.3) | copy-start | bytes 786436
  0.6 52.1 %copy-start = (f32[2,256,4,256]{3,2,1,0:T(4,128)S(1)}, f32[2,256,4,256]{3,2,1,0:T(4,128)}, u32[]{:S(2)}) copy-start(f32[2,256,4,256]{3,2,1,0:T(4,128)} %param.3) | copy-start | bytes 6291460
  0.6 18.0 %collective-permute-start = (f32[2,16,256]{2,1,0:T(8,128)}, f32[2,16,256]{2,1,0:T(8,128)S(1)}, u32[]{:S(2)}, u32[]{:S(2)}) collective-permute-start(f32[2,16,256]{2,1,0:T(8,128)} %bitcast.18), channel_id=1, source_target_pairs={{0,0},{1,32},{2,64},{3,96},{4,128},{5,160},{6,192},{7,224},{8,256}... | collective-permute-start | bytes 98312 | tf_op jit(solution)/shard_map/ppermute | solution.py:84
  19.5 23.7 %all-to-all-start = ((f32[16,2,16,256]{3,2,1,0:T(8,128)}), f32[16,2,16,256]{3,2,1,0:T(8,128)S(1)}, u32[]{:S(2)}, u32[]{:S(2)}) async-start(f32[16,2,16,256]{3,2,1,0:T(8,128)} %broadcast_in_dim.10), calls=%async_computation | async-start | bytes 1048576 | tf_op jit(solution)/shard_map/all_to_all | solution.py:88
  43.2 9.5 %collective-permute-start.1 = (f32[16,2,16,256]{3,2,1,0:T(8,128)S(1)}, f32[16,2,16,256]{3,2,1,0:T(8,128)}, u32[]{:S(2)}, u32[]{:S(2)}) collective-permute-start(f32[16,2,16,256]{3,2,1,0:T(8,128)S(1)} %all-to-all-done.mine_ref), channel_id=1, source_target_pairs={{0,16},{16,0},{1,17},{17,1},{2,18},{18,2},{3,19},{19,3},{4,20},{20... | collective-permute-start | bytes 1572872 | tf_op jit(solution)/shard_map/ppermute | solution.py:91

commit v5 on v4

--- a/solution.py
+++ b/solution.py
@@ -38,15 +38,21 @@
     return dot(left[0], right[0]) + (dot(left[0], right[1]) + dot(left[1], right[0]))
 
 
-def own_kernel(at_ref, rows_ref, mine_ref, inverse_ref, high_ref, low_ref, right_high_ref, right_low_ref, panel_ref):
+def own_kernel(at_ref, rows_ref, inverse_ref, high_ref, low_ref, panel_ref):
     inverse = split(inverse_ref[...])
     start = pl.multiple_of(at_ref[0] * 16, 16)
     for t in range(2):
-        rows = split(rows_ref[:, t].reshape(256, 256))
-        high_ref[t], low_ref[t] = split(product(inverse, rows).T)
-        panel_ref[t] = product(split(inverse_ref[pl.ds(start, 16), :]), rows)
+        factor = product(inverse, split(rows_ref[:, t].reshape(256, 256)))
+        high_ref[t], low_ref[t] = split(factor.T)
+        panel_ref[t] = product(
+            split(inverse_ref[pl.ds(start, 16), :]), split(rows_ref[:, t].reshape(256, 256))
+        )
+
+
+def column_kernel(mine_ref, inverse_ref, high_ref, low_ref):
+    inverse = split(inverse_ref[...])
     for t in range(2):
-        right_high_ref[t], right_low_ref[t] = split(product(inverse, split(mine_ref[:, t].reshape(256, 256))))
+        high_ref[t], low_ref[t] = split(product(inverse, split(mine_ref[:, t].reshape(256, 256))))
 
 
 def update_kernel(at_ref, trailing_ref, high_ref, low_ref, mine_high, mine_low, other_ref, inverse_ref, out_ref, right_high, right_low, done, sems):
@@ -87,19 +93,30 @@
     many = jnp.broadcast_to(sent[None], (16, 2, 16, 256))
     mine = lax.all_to_all(many, ("z", "yl"), 0, 0, tiled=True)
     own = lax.all_gather(quarter, "x", axis=0, tiled=True)
-    mine, own = lax.optimization_barrier((mine, own))
-    other = lax.ppermute(mine, "core", [(0, 1), (1, 0)])
 
     smem = pl.BlockSpec(memory_space=pltpu.SMEM)
     vmem = pl.BlockSpec(memory_space=pltpu.VMEM)
-    square = jax.ShapeDtypeStruct((2, 256, 256), jnp.bfloat16)
-    high, low, right_high, right_low, factor_panel = pl.pallas_call(
+    high, low, factor_panel = pl.pallas_call(
         own_kernel,
-        out_shape=[square] * 4 + [jax.ShapeDtypeStruct((2, 16, 256), jnp.float32)],
-        in_specs=[smem, vmem, vmem, vmem],
-        out_specs=[vmem] * 5,
+        out_shape=[
+            jax.ShapeDtypeStruct((2, 256, 256), jnp.bfloat16),
+            jax.ShapeDtypeStruct((2, 256, 256), jnp.bfloat16),
+            jax.ShapeDtypeStruct((2, 16, 256), jnp.float32),
+        ],
+        in_specs=[smem, vmem, vmem],
+        out_specs=[vmem, vmem, vmem],
         compiler_params=pltpu.CompilerParams(vmem_limit_bytes=32 * 1024 * 1024),
-    )(at, own, mine, factor_inverse)
+    )(at, own, factor_inverse)
+
+    mine, high, low = lax.optimization_barrier((mine, high, low))
+    other = lax.ppermute(mine, "core", [(0, 1), (1, 0)])
+    mine_high, mine_low = pl.pallas_call(
+        column_kernel,
+        out_shape=[jax.ShapeDtypeStruct((2, 256, 256), jnp.bfloat16)] * 2,
+        in_specs=[vmem, vmem],
+        out_specs=[vmem, vmem],
+        compiler_params=pltpu.CompilerParams(vmem_limit_bytes=32 * 1024 * 1024),
+    )(mine, factor_inverse)
 
     whole = trailing.reshape(2, 256, 4, 2, 128).swapaxes(2, 3).reshape(2, 256, 8, 128)
     updated = pl.pallas_call(
@@ -114,7 +131,7 @@
             pltpu.SemaphoreType.DMA((512 // 64,)),
         ],
         compiler_params=pltpu.CompilerParams(vmem_limit_bytes=32 * 1024 * 1024),
-    )(at, whole, high, low, right_high, right_low, other, factor_inverse)
+    )(at, whole, high, low, mine_high, mine_low, other, factor_inverse)
     updated = updated.reshape(2, 256, 2, 4, 128).swapaxes(2, 3).reshape(2, 256, 4, 256)
     return updated, jnp.swapaxes(factor_panel, 1, 2)
 

time: 57.3 us -> 57.4 us (level); the launches traced: 56.3 us -> 57.2 us
  waiting for transfers between devices: 0.01 us -> 1.13 us
    ppermute x1, waiting for transfers between devices: 0.01 us -> 1.12 us  [on_device(): other = lax.ppermute(mine, 'core', [(0, 1), (1, 0)])]
    pallas_call x1 -> x2, Pallas kernels: 1.72 us -> 1.98 us  [the longest x1 1.6 us: on_device(): pl.pallas_call(own_kernel, out_shape=[jax.ShapeDtypeStruct((2, 256, 256),...]
  transfers between devices with their start and end apart: 3 -> 3, of which waited for: 0 -> 1; matrix products, arithmetic and copies ran while one was open for 0% -> 0% of each run, Pallas kernels for 3% -> 3%
where the time goes in v5:
time: 57.4 us; the launch traced here: 57.2 us
  blocking collectives  27.9 us (49%)
  starting transfers between devices  21.5 us (37%)
  Pallas kernels  5.05 us (9%)
  waiting for transfers between devices  1.13 us (2%)
  local copies, waits for them, and re-layouts  0.86 us (1%)
  between operations  0.69 us (1%)
    all_gather x1, blocking collectives, on_device(): own = lax.all_gather(quarter, 'x', axis=0, tiled=True)  15.6 us
    all_to_all x1, starting transfers between devices, on_device(): mine = lax.all_to_all(many, ('z', 'yl'), 0, 0, tiled=True)  8.04 us
    ppermute x1, starting transfers between devices, on_device(): other = lax.ppermute(mine, 'core', [(0, 1), (1, 0)])  7.7 us
    all_gather x1, blocking collectives, gather_pairs(): lax.all_gather(block, axis, axis=0, tiled=True, axis_index_groups=[[0, 3]...  7.62 us
    ppermute x1, starting transfers between devices, on_device(): sent = lax.ppermute(sliver, AXES, to_columns())  5.74 us
    all_gather x1, blocking collectives, gather_pairs(): lax.all_gather(block, axis, axis=0, tiled=True, axis_index_groups=[[0, 1]...  4.65 us
    pallas_call x1, Pallas kernels, on_device(): pl.pallas_call(update_kernel, out_shape=jax.ShapeDtypeStruct((2, 256, 8,...  3.07 us
    pallas_call x1, Pallas kernels, on_device(): pl.pallas_call(own_kernel, out_shape=[jax.ShapeDtypeStruct((2, 256, 256),...  1.6 us
  transfers between devices with their start and end apart: 3, of which 1 were waited for; matrix products, arithmetic and copies ran while one was open for 0% of the time, Pallas kernels for 3%

profile of v5, /device:TPU:1, one launch (start us, length us, event | category | flops | bytes accessed | tf_op | source)
XLA Modules:
  0.0 57.2 jit_solution(2273911912675241484)
XLA Ops:
  0.6 0.0 copy-start
  0.6 0.0 copy-start.1
  0.6 5.7 %collective-permute-start = (f32[2,16,256]{2,1,0:T(8,128)}, f32[2,16,256]{2,1,0:T(8,128)S(1)}, u32[]{:S(2)}, u32[]{:S(2)}) collective-permute-start(f32[2,16,256]{2,1,0:T(8,128)} %bitcast.18), channel_id=1, source_target_pairs={{0,0},{1,32},{2,64},{3,96},{4,128},{5,160},{6,192},{7,224},{8,256}... | collective-permute-start | bytes 98312 | tf_op jit(solution)/shard_map/ppermute | solution.py:90
  6.4 4.7 %all-gather = f32[4,16,256]{2,1,0:T(8,128)S(1)} all-gather(f32[2,16,256]{2,1,0:T(8,128)} %bitcast.19), channel_id=2, replica_groups={{0,1},{2,3},{4,5},{6,7},{8,9},{10,11},{12,13},{14,15},{16,17},{18,19},{..., dimensions={0}, use_global_device_ids=true | all-gather | bytes 98304 | tf_op jit(solution)/shard_map/all_gather | solution.py:26
  11.1 7.6 %all_gather.10 = f32[4,2,16,256]{3,2,1,0:T(8,128)S(1)} all-gather(f32[2,2,16,256]{3,2,1,0:T(8,128)S(1)} %bitcast.17), channel_id=1, replica_groups={{0,3},{1,2},{4,7},{5,6},{8,11},{9,10},{12,15},{13,14},{16,19},{17,18},{..., dimensions={0}, use_global_device_ids=true | all-gather | bytes 196608 | tf_op jit(solution)/shard_map/all_gather | solution.py:27
  18.7 0.0 collective-permute-done
  18.7 0.9 %broadcast_in_dim.10 = f32[16,2,16,256]{3,2,1,0:T(8,128)} broadcast(f32[2,16,256]{2,1,0:T(8,128)S(1)} %collective-permute-done), dimensions={1,2,3} | broadcast | bytes 557056 | tf_op jit(solution)/shard_map/broadcast_in_dim | solution.py:93
  19.5 8.0 %all-to-all-start = ((f32[16,2,16,256]{3,2,1,0:T(8,128)}), f32[16,2,16,256]{3,2,1,0:T(8,128)S(1)}, u32[]{:S(2)}, u32[]{:S(2)}) async-start(f32[16,2,16,256]{3,2,1,0:T(8,128)} %broadcast_in_dim.10), calls=%async_computation | async-start | bytes 1048576 | tf_op jit(solution)/shard_map/all_to_all | solution.py:94
  27.6 0.1 pad_add_fusion.at_ref
  27.7 15.6 %all_gather.11.rows_ref = f32[16,2,16,256]{3,2,1,0:T(8,128)S(1)} all-gather(f32[4,2,16,256]{3,2,1,0:T(8,128)S(1)} %all_gather.10), channel_id=1, replica_groups=mesh['z'=8,'yl'=2,'core'=2,'x'=4,'yh'=4] {'x'}, dimensions={0}, use_global_device_ids=true | all-gather | bytes 655360 | tf_op jit(solution)/shard_map/all_gather | solution.py:95
  43.3 0.0 copy-done
  43.3 1.6 %shard_map.50 = (bf16[2,256,256]{2,1,0:T(8,128)(2,1)S(1)}, bf16[2,256,256]{2,1,0:T(8,128)(2,1)S(1)}, f32[2,16,256]{2,1,0:T(8,128)}) custom-call(s32[2]{0:T(128)S(1)} %pad_add_fusion.at_ref, f32[16,2,16,256]{3,2,1,0:T(8,128)S(1)} %all_gather.11.rows_ref, f32[256,256]{1,0:T(8,128)S(1)} %copy-done), custom_call_target="tpu_custom_call" | custom-call | tf_op jit(solution)/shard_map/pallas_call | solution.py:99
  44.9 0.0 all-to-all-done.mine_ref
  44.9 7.7 %collective-permute-start.1 = (f32[16,2,16,256]{3,2,1,0:T(8,128)S(1)}, f32[16,2,16,256]{3,2,1,0:T(8,128)S(1)}, u32[]{:S(2)}, u32[]{:S(2)}) collective-permute-start(f32[16,2,16,256]{3,2,1,0:T(8,128)S(1)} %all-to-all-done.mine_ref), channel_id=1, source_target_pairs={{0,16},{16,0},{1,17},{17,1},{2,18},{18,2},{3,19},{19,3},{4,20},{20... | collective-permute-start | bytes 1572872 | tf_op jit(solution)/shard_map/ppermute | solution.py:112
  52.6 0.4 shard_map.51
  53.0 1.1 %collective-permute-done.1.other_ref = f32[16,2,16,256]{3,2,1,0:T(8,128)S(1)} collective-permute-done((f32[16,2,16,256]{3,2,1,0:T(8,128)S(1)}, f32[16,2,16,256]{3,2,1,0:T(8,128)S(1)}, u32[]{:S(2)}, u32[]{:S(2)}) %collective-permute-start.1) | collective-permute-done | bytes 524320 | tf_op jit(solution)/shard_map/ppermute | solution.py:112
  54.1 0.0 copy-done.1
  54.1 3.1 %shard_map.52 = f32[2,256,8,128]{3,2,1,0:T(8,128)} custom-call(s32[2]{0:T(128)S(1)} %pad_add_fusion.at_ref, f32[2,256,8,128]{3,2,1,0:T(8,128)S(1)} %bitcast.15, bf16[2,256,256]{2,1,0:T(8,128)(2,1)S(1)} %get-tuple-element.16.high_ref, bf16[2,256,256]{2,1,0:T(8,128)(2,1)S(1)} %get-tuple-element.17.low_ref, ...), custom_call_target="tpu_custom_call" | custom-call | tf_op jit(solution)/shard_map/pallas_call | solution.py:122
Async XLA Ops:
  0.6 42.6 %copy-start = (f32[256,256]{1,0:T(8,128)S(1)}, f32[256,256]{1,0:T(8,128)}, u32[]{:S(2)}) copy-start(f32[256,256]{1,0:T(8,128)} %inverse_ref.5) | copy-start | bytes 786436
  0.6 53.5 %copy-start.1 = (f32[2,256,4,256]{3,2,1,0:T(4,128)S(1)}, f32[2,256,4,256]{3,2,1,0:T(4,128)}, u32[]{:S(2)}) copy-start(f32[2,256,4,256]{3,2,1,0:T(4,128)} %param.3) | copy-start | bytes 6291460
  0.6 18.0 %collective-permute-start = (f32[2,16,256]{2,1,0:T(8,128)}, f32[2,16,256]{2,1,0:T(8,128)S(1)}, u32[]{:S(2)}, u32[]{:S(2)}) collective-permute-start(f32[2,16,256]{2,1,0:T(8,128)} %bitcast.18), channel_id=1, source_target_pairs={{0,0},{1,32},{2,64},{3,96},{4,128},{5,160},{6,192},{7,224},{8,256}... | collective-permute-start | bytes 98312 | tf_op jit(solution)/shard_map/ppermute | solution.py:90
  19.5 25.3 %all-to-all-start = ((f32[16,2,16,256]{3,2,1,0:T(8,128)}), f32[16,2,16,256]{3,2,1,0:T(8,128)S(1)}, u32[]{:S(2)}, u32[]{:S(2)}) async-start(f32[16,2,16,256]{3,2,1,0:T(8,128)} %broadcast_in_dim.10), calls=%async_computation | async-start | bytes 1048576 | tf_op jit(solution)/shard_map/all_to_all | solution.py:94
  44.9 9.2 %collective-permute-start.1 = (f32[16,2,16,256]{3,2,1,0:T(8,128)S(1)}, f32[16,2,16,256]{3,2,1,0:T(8,128)S(1)}, u32[]{:S(2)}, u32[]{:S(2)}) collective-permute-start(f32[16,2,16,256]{3,2,1,0:T(8,128)S(1)} %all-to-all-done.mine_ref), channel_id=1, source_target_pairs={{0,16},{16,0},{1,17},{17,1},{2,18},{18,2},{3,19},{19,3},{4,20},{20... | collective-permute-start | bytes 1572872 | tf_op jit(solution)/shard_map/ppermute | solution.py:112
